TPU v7x, 32 devices: a whole 2x2x4 slice. The times are simulated.
32 devices in a mesh: dp: 8 (over z, x), seq: 4 (over y, core).
Axes of the slice: x: 2, y: 2, z: 4, core: 2. Of those that a mesh axis runs over, the one named last changes fastest.
Arguments:
- queries: bfloat16 [8, 512, 768], P('dp', 'seq'), may hold values from -720 to 720
- key_rows: bfloat16 [8, 512, 768], P('dp', 'seq'), may hold values from -7 to 7
- value_rows: bfloat16 [8, 512, 768], P('dp', 'seq'), may hold values from -6 to 6
- conv_weight: bfloat16 [768, 3, 768], replicated, may hold values from -0.125 to 0.125
- output_gradient: bfloat16 [8, 512, 768], P('dp', 'seq'), may hold values from -6 to 6
Outputs:
- conv_out: bfloat16 [8, 512, 768], P('dp', 'seq')
- grad_queries: bfloat16 [8, 512, 768], P('dp', 'seq')
- grad_keys: bfloat16 [8, 512, 768], P('dp', 'seq')
- grad_values: bfloat16 [8, 512, 768], P('dp', 'seq')
- grad_weight: float32 [768, 3, 768], P('dp', None, 'seq')
All inputs are finite; a program needn't handle non-finite values.
Results may differ from a plain program's by a relative error of at most 0.014.
Values may be sent and summed in bfloat16 or wider, within the bound.
A program may use at most 64 MiB of HBM per device.

v0:
```python
import math

import jax
import jax.numpy as jnp
from jax import lax
from jax.sharding import PartitionSpec as P

HEAD_DIM = 192
TAPS = 3
DILATION_STEP = 32


tanh_scale = 0.7978845608028654
cubic_term = 0.044715
norm_epsilon = 1e-06


def padded(block, sides, width):
    for axis, dim in sides:
        count = lax.axis_size(axis)
        forward = [(i, i + 1) for i in range(count - 1)]
        backward = [(target, source) for source, target in forward]
        low = lax.ppermute(
            lax.slice_in_dim(block, block.shape[dim] - width, None, axis=dim), axis, forward
        )
        high = lax.ppermute(lax.slice_in_dim(block, 0, width, axis=dim), axis, backward)
        block = jnp.concatenate([low, block, high], axis=dim)
    return block


def gelu_pair(value):
    inner = tanh_scale * (value + cubic_term * value * value * value)
    tangent = jnp.tanh(inner)
    result = 0.5 * value * (1.0 + tangent)
    slope = 0.5 * (1.0 + tangent) + 0.5 * value * (1.0 - tangent * tangent) * tanh_scale * (
        1.0 + 3.0 * cubic_term * value * value
    )
    return (result, slope)


def split_heads(matrix):
    return matrix.reshape(matrix.shape[0], matrix.shape[1] // HEAD_DIM, HEAD_DIM)


def attend_forward(query, keys, values):
    query_count, features = query.shape
    inverse = 1.0 / math.sqrt(HEAD_DIM)
    scores = (
        jnp.einsum(
            "qhd,khd->hqk",
            split_heads(query),
            split_heads(keys),
            preferred_element_type=jnp.float32,
        )
        * inverse
    )
    soft_exact = jax.nn.softmax(scores, axis=-1)
    soft_rounded = soft_exact.astype(jnp.bfloat16)
    attended = jnp.einsum(
        "hqk,khd->qhd", soft_rounded, split_heads(values), preferred_element_type=jnp.float32
    )
    return (soft_exact, soft_rounded, attended.reshape(query_count, features).astype(jnp.bfloat16))


def score_grads(values, soft_exact, grad_out):
    inverse = 1.0 / math.sqrt(HEAD_DIM)
    grad_soft = jnp.einsum(
        "qhd,khd->hqk",
        split_heads(grad_out),
        split_heads(values),
        preferred_element_type=jnp.float32,
    )
    row_inner = jnp.sum(grad_soft * soft_exact, axis=-1, keepdims=True)
    return (soft_exact * (grad_soft - row_inner) * inverse).astype(jnp.bfloat16)


def query_side(grad_scores, keys):
    features = keys.shape[1]
    grad_queries = jnp.einsum(
        "hqk,khd->qhd", grad_scores, split_heads(keys), preferred_element_type=jnp.float32
    )
    return grad_queries.reshape(grad_queries.shape[0], features)


def key_side(score_part, soft_part, query, grad_out):
    features = query.shape[1]
    grad_keys = jnp.einsum(
        "hqk,qhd->khd", score_part, split_heads(query), preferred_element_type=jnp.float32
    )
    grad_values = jnp.einsum(
        "hqk,qhd->khd", soft_part, split_heads(grad_out), preferred_element_type=jnp.float32
    )
    row_total = grad_keys.shape[0]
    return jnp.concatenate(
        [grad_keys.reshape(row_total, features), grad_values.reshape(row_total, features)], axis=1
    )


def body(queries, key_rows, value_rows, conv_weight, output_gradient):
    local_shard_rows = queries.shape[1]
    features = queries.shape[2]
    total_rows = lax.axis_size("dp") * lax.axis_size("seq") * local_shard_rows
    grad_scale = 1.0 / math.sqrt(total_rows)
    padded_gradient = padded(output_gradient, (("seq", 1),), DILATION_STEP)
    whole_keys, whole_values = (
        lax.all_gather(key_rows, "seq", axis=1, tiled=True),
        lax.all_gather(value_rows, "seq", axis=1, tiled=True),
    )
    soft_exact, soft_rounded, attended = attend_forward(queries[0], whole_keys[0], whole_values[0])
    att_full = attended.astype(jnp.float32)
    mean_square = jnp.mean(att_full * att_full, axis=-1, keepdims=True)
    norm_factor = lax.rsqrt(mean_square + norm_epsilon)
    normed = att_full * norm_factor
    gelu_value, gelu_slope = gelu_pair(normed)
    activation_output = gelu_value.astype(jnp.bfloat16)
    padded_input = padded(activation_output[None], (("seq", 1),), DILATION_STEP)[0]
    incoming_gradient = output_gradient[0]
    row_gradient = padded_gradient[0]
    conv_sum = jnp.zeros((local_shard_rows, conv_weight.shape[2]), jnp.float32)
    grad_acted = jnp.zeros((local_shard_rows, features), jnp.float32)
    for kernel_tap_index in range(TAPS):
        shifted_input = padded_input[
            kernel_tap_index * DILATION_STEP : kernel_tap_index * DILATION_STEP + local_shard_rows
        ]
        conv_sum = conv_sum + jnp.dot(
            shifted_input, conv_weight[:, kernel_tap_index, :], preferred_element_type=jnp.float32
        )
        reverse_rows = row_gradient[
            (2 - kernel_tap_index) * DILATION_STEP : (2 - kernel_tap_index) * DILATION_STEP
            + local_shard_rows
        ]
        grad_acted = grad_acted + jnp.einsum(
            "pc,dc->pd",
            reverse_rows,
            conv_weight[:, kernel_tap_index, :],
            preferred_element_type=jnp.float32,
        )
    conv_out = conv_sum.astype(jnp.bfloat16)
    grad_normed = grad_acted * gelu_slope
    mean_inner = jnp.mean(grad_normed * normed, axis=-1, keepdims=True)
    grad_attended = (norm_factor * (grad_normed - normed * mean_inner)).astype(jnp.bfloat16)
    grad_scores = score_grads(whole_values[0], soft_exact, grad_attended)
    grad_queries = query_side(grad_scores, whole_keys[0]).astype(jnp.bfloat16)
    grad_pair = lax.psum_scatter(
        key_side(grad_scores, soft_rounded, queries[0], grad_attended),
        "seq",
        scatter_dimension=0,
        tiled=True,
    )
    grad_keys = grad_pair[:, :features].astype(jnp.bfloat16)
    grad_values = grad_pair[:, features:].astype(jnp.bfloat16)
    grad_queries = grad_queries[None]
    grad_keys = grad_keys[None]
    grad_values = grad_values[None]
    tap_terms = [
        jnp.einsum(
            "pd,pc->dc",
            padded_input[
                kernel_tap_index * DILATION_STEP : kernel_tap_index * DILATION_STEP
                + local_shard_rows
            ],
            incoming_gradient,
            preferred_element_type=jnp.float32,
        )
        for kernel_tap_index in range(TAPS)
    ]
    local_term = jnp.stack(tap_terms, axis=1) * grad_scale
    partial_value = lax.psum_scatter(
        local_term.astype(jnp.bfloat16), "seq", scatter_dimension=2, tiled=True
    ).astype(jnp.float32)
    grad_weight = lax.psum_scatter(partial_value, "dp", scatter_dimension=0, tiled=True)
    return (conv_out[None], grad_queries, grad_keys, grad_values, grad_weight)


def solution(mesh):
    return jax.shard_map(
        body,
        mesh=mesh,
        in_specs=(
            P("dp", "seq", None),
            P("dp", "seq", None),
            P("dp", "seq", None),
            P(),
            P("dp", "seq", None),
        ),
        out_specs=(
            P("dp", "seq", None),
            P("dp", "seq", None),
            P("dp", "seq", None),
            P("dp", "seq", None),
            P("dp", None, "seq"),
        ),
        check_vma=False,
    )
```

profile of v0, /device:TPU:0, one launch (start us, length us, event | category | flops | bytes accessed | tf_op | source)
XLA Modules:
  0.0 214.0 jit_solution(8426501292931236592)
XLA Ops:
  7.2 0.0 reduce-scatter.10.cloned.1.call-start
  7.2 1.1 copy.28
  8.3 0.0 copy-start.14
  8.4 10.3 %all_gather.6 = bf16[1,512,768]{2,1,0:T(8,128)(2,1)S(1)} all-gather(bf16[1,128,768]{2,1,0:T(8,128)(2,1)} %param.6), channel_id=1, replica_groups=mesh['dp'=8,'seq'=4] {'seq'}, dimensions={1}, use_global_device_ids=true | all-gather | bytes 983040 | tf_op jit(solution)/shard_map/all_gather | solution.py:106
  18.6 0.3 copy.29
  18.9 8.7 %all_gather.7 = bf16[1,512,768]{2,1,0:T(8,128)(2,1)S(1)} all-gather(bf16[1,128,768]{2,1,0:T(8,128)(2,1)S(1)} %copy-done.18), channel_id=1, replica_groups=mesh['dp'=8,'seq'=4] {'seq'}, dimensions={1}, use_global_device_ids=true | all-gather | bytes 983040 | tf_op jit(solution)/shard_map/all_gather | solution.py:107
  27.7 0.3 copy.30
  28.0 1.6 fusion.94
  29.5 0.8 multiply_reduce_fusion.2
  30.4 0.2 fusion.46
  30.5 0.0 copy-start
  30.5 0.1 fusion.93
  30.7 2.3 %collective-permute-start = (bf16[1,32,768]{1,2,0:T(8,128)(2,1)S(1)}, bf16[1,32,768]{1,2,0:T(8,128)(2,1)S(1)}, u32[]{:S(2)}, u32[]{:S(2)}) collective-permute-start(bf16[1,32,768]{1,2,0:T(8,128)(2,1)S(1)} %get-tuple-element.24), channel_id=1, source_target_pairs={{0,1},{1,2},{2,3},{4,5},{5,6},{6,7},{8,9},{9,10},{10,11},{12,13},{... | collective-permute-start | bytes 147464 | tf_op jit(solution)/shard_map/ppermute | solution.py:23
  32.9 1.3 collective-permute-start.1
  34.3 0.5 convolution_bitcast_fusion.1
  34.7 0.0 collective-permute-done
  34.7 0.0 copy-start.12
  34.8 0.5 convolution_bitcast_fusion.2
  35.3 1.3 collective-permute-done.1
  36.6 0.7 copy-done.16
  37.3 0.5 convolution_bitcast_fusion
  37.9 0.7 fusion.2
  38.5 5.7 %copy.36 = bf16[768,3,768]{0,1,2:T(4,128)(2,1)} copy(bf16[768,3,768]{2,0,1:T(8,128)(2,1)S(1)} %fusion.2) | data formatting | bytes 7077888
  44.2 4.9 %copy.38 = bf16[96,8,3,768]{3,1,2,0:T(8,128)(2,1)} copy(bf16[96,8,3,768]{3,2,1,0:T(4,128)(2,1)} %bitcast.104) | data formatting | bytes 7077888
  49.1 0.0 reduce-scatter.10.cloned.1.call-update
  49.1 0.0 reduce-scatter.6.cloned.1.call-start
  49.1 0.8 copy-done.3
  50.0 1.3 collective-permute-start.2
  51.3 6.7 %collective-permute-start.3 = (bf16[1,32,768]{2,1,0:T(8,128)(2,1)S(1)}, bf16[1,32,768]{2,1,0:T(8,128)(2,1)S(1)}, u32[]{:S(2)}, u32[]{:S(2)}) collective-permute-start(bf16[1,32,768]{2,1,0:T(8,128)(2,1)S(1)} %get-tuple-element.23), channel_id=1, source_target_pairs={{0,1},{1,2},{2,3},{4,5},{5,6},{6,7},{8,9},{9,10},{10,11},{12,13},{... | collective-permute-start | bytes 147464 | tf_op jit(solution)/shard_map/ppermute | solution.py:23
  58.0 2.1 %fusion.16 = f32[128,768]{1,0:T(8,128)S(1)} fusion(bf16[768,3,768]{2,0,1:T(8,128)(2,1)} %param.8, bf16[1,128,768]{2,1,0:T(8,128)(2,1)S(1)} %copy-done.3), kind=kOutput, calls=%fused_computation.24 | convolution fusion | flops 150994944 | bytes 1769472 | tf_op jit(solution)/shard_map/pc,dc->pd/dot_general | solution.py:132
  60.1 0.2 copy.31
  60.3 0.0 collective-permute-done.3
  60.3 2.1 %fusion.12 = f32[128,768]{1,0:T(8,128)S(1)} fusion(bf16[768,3,768]{2,0,1:T(8,128)(2,1)} %param.8, bf16[1,128,768]{2,1,0:T(8,128)(2,1)S(1)} %copy-done.3, bf16[1,32,768]{2,1,0:T(8,128)(2,1)S(1)} %collective-permute-done.3), kind=kOutput, calls=%fused_computation.20 | convolution fusion | flops 151388160 | bytes 1818624 | tf_op jit(solution)/shard_map/pc,dc->pd/dot_general | solution.py:132
  62.5 0.0 collective-permute-done.2
  62.5 2.1 multiply_reduce_fusion.1
  64.6 0.0 copy-start.15
  64.6 0.1 multiply_convert_fusion
  64.8 0.2 copy.32
  64.9 0.3 fusion.95
  65.3 1.0 copy-done.11
  66.3 5.4 %fusion.35 = f32[4,512,192]{1,2,0:T(8,128)} fusion(bf16[128,4,192]{0,2,1:T(8,128)(2,1)S(1)} %bitcast.121, f32[4,128,512]{2,1,0:T(8,128)S(1)} %fusion.95, f32[4,128,512]{2,1,0:T(8,128)} %get-tuple-element.27, f32[4,128]{1,0:T(4,128)S(1)} %get-tuple-element.26), kind=kOutput, calls=%fused_computation.41 | convolution fusion | flops 102499328 | bytes 3868672 | tf_op jit(solution)/shard_map/hqk,qhd->khd/dot_general | solution.py:87
  71.7 2.0 copy.33
  73.7 1.9 fusion.57
  75.6 1.9 copy.34
  77.5 2.1 pad_maximum_fusion
  79.6 0.0 reduce-scatter.6.cloned.1.call-update
  79.6 0.2 reduce-scatter.8.cloned.1.call-start
  79.8 13.9 %reduce-scatter.10.cloned.1.call-done = bf16[192,2304]{1,0:T(8,128)(2,1)} async-done(((bf16[768,2304]{1,0:T(8,128)(2,1)}), bf16[192,2304]{1,0:T(8,128)(2,1)}) %reduce-scatter.10.cloned.1.call-update) | async-done | bytes 884752
  93.7 2.2 %reshape.218 = bf16[192,3,768]{2,1,0:T(4,128)(2,1)S(1)} reshape(bf16[192,2304]{1,0:T(8,128)(2,1)} %reduce-scatter.10.cloned.1.call-done) | data formatting | bytes 1769472
  95.9 0.9 copy.37
  96.8 1.7 convert_element_type.174
  98.5 0.0 reduce-scatter.8.cloned.1.call-update
  98.5 1.8 fusion.18
  100.3 0.0 copy-start.1
  100.3 0.0 copy-start.17
  100.3 5.2 %convolution_convert_fusion = bf16[4,128,192]{1,2,0:T(8,128)(2,1)S(1)} fusion(bf16[512,4,192]{0,2,1:T(8,128)(2,1)S(1)} %bitcast.114, f32[4,128,512]{2,1,0:T(8,128)} %copy-done.11, f32[4,128,512]{2,1,0:T(8,128)} %get-tuple-element.27, f32[4,128]{1,0:T(4,128)S(1)} %get-tuple-element.26), kind=kOutput, calls=%fused_computation.31 | convolution fusion | flops 102597632 | bytes 3082240 | tf_op jit(solution)/shard_map/hqk,khd->qhd/dot_general | solution.py:79
  105.5 0.0 copy-start.13
  105.5 0.8 copy.35
  106.4 1.8 fusion.14
  108.2 2.4 %fusion.26 = bf16[1,128,768]{2,1,0:T(8,128)(2,1)} fusion(f32[128,768]{1,0:T(8,128)S(1)} %fusion.14, f32[128,768]{1,0:T(8,128)S(1)} %fusion.18, bf16[768,3,768]{2,0,1:T(8,128)(2,1)} %param.8, bf16[1,128,768]{1,2,0:T(8,128)(2,1)S(1)} %copy-done.1, bf16[1,32,768]{1,2,0:T(8,128)(2,1)S(1)} %copy-done.13), kind=kOutput, calls=%fused_computation.34 | convolution fusion | flops 151683072 | bytes 2408448 | tf_op jit(solution)/shard_map/dot_general | solution.py:125
  110.6 23.8 %reduce-scatter.6.cloned.1.call-done = f32[128,1536]{1,0:T(8,128)} async-done(((f32[512,1536]{1,0:T(8,128)}), f32[128,1536]{1,0:T(8,128)}) %reduce-scatter.6.cloned.1.call-update) | async-done | bytes 786448 | tf_op jit(solution)/shard_map/reduce_scatter | solution.py:144
  134.4 1.2 convert.10
  135.6 0.8 slice_bitcast_fusion
  136.4 71.1 %reduce-scatter.8.cloned.1.call-done = f32[96,3,192]{2,0,1:T(8,128)} async-done(((f32[768,3,192]{2,0,1:T(8,128)}), f32[96,3,192]{2,0,1:T(8,128)}) %reduce-scatter.8.cloned.1.call-update) | async-done | bytes 221200 | tf_op jit(solution)/shard_map/reduce_scatter | solution.py:171
  (31 shorter events, 0.1 us)
Async XLA Ops:
  7.2 11.8 %copy-start.18 = (bf16[1,128,768]{2,1,0:T(8,128)(2,1)S(1)}, bf16[1,128,768]{2,1,0:T(8,128)(2,1)}, u32[]{:S(2)}) copy-start(bf16[1,128,768]{2,1,0:T(8,128)(2,1)} %param.7) | copy-start | bytes 589828
  7.2 86.5 %reduce-scatter.10.cloned.1.call-start = ((), (), s32[]{:S(2)}) async-start(), calls=%async_computation.5 | async-start | bytes 4423680
  8.3 21.2 %copy-start.14 = (bf16[1,128,768]{1,2,0:T(8,128)(2,1)}, bf16[1,128,768]{1,2,0:T(8,128)(2,1)S(1)}, u32[]{:S(2)}) copy-start(bf16[1,128,768]{1,2,0:T(8,128)(2,1)S(1)} %copy.28) | copy-start | bytes 589828
  18.9 11.4 %copy-start.6 = (bf16[1,512,768]{1,2,0:T(8,128)(2,1)}, bf16[1,512,768]{1,2,0:T(8,128)(2,1)S(1)}, u32[]{:S(2)}) copy-start(bf16[1,512,768]{1,2,0:T(8,128)(2,1)S(1)} %copy.29) | copy-start | bytes 2359300
  28.0 2.4 %copy-start.9 = (bf16[1,512,768]{1,2,0:T(8,128)(2,1)}, bf16[1,512,768]{1,2,0:T(8,128)(2,1)S(1)}, u32[]{:S(2)}) copy-start(bf16[1,512,768]{1,2,0:T(8,128)(2,1)S(1)} %copy.30) | copy-start | bytes 2359300
  29.5 4.7 %copy-start.2 = (bf16[1,128,768]{2,1,0:T(8,128)(2,1)S(1)}, bf16[1,128,768]{2,1,0:T(8,128)(2,1)}, u32[]{:S(2)}) copy-start(bf16[1,128,768]{2,1,0:T(8,128)(2,1)} %param.9) | copy-start | bytes 589828
  30.4 4.9 %copy-start.4 = (f32[4,128,192]{1,2,0:T(8,128)}, f32[4,128,192]{1,2,0:T(8,128)S(1)}, u32[]{:S(2)}) copy-start(f32[4,128,192]{1,2,0:T(8,128)S(1)} %get-tuple-element.29) | copy-start | bytes 1179652
  30.5 6.1 %copy-start = (bf16[1,128,768]{1,2,0:T(8,128)(2,1)}, bf16[1,128,768]{1,2,0:T(8,128)(2,1)S(1)}, u32[]{:S(2)}) copy-start(bf16[1,128,768]{1,2,0:T(8,128)(2,1)S(1)} %fusion.46) | copy-start | bytes 589828
  30.7 4.1 %collective-permute-start = (bf16[1,32,768]{1,2,0:T(8,128)(2,1)S(1)}, bf16[1,32,768]{1,2,0:T(8,128)(2,1)S(1)}, u32[]{:S(2)}, u32[]{:S(2)}) collective-permute-start(bf16[1,32,768]{1,2,0:T(8,128)(2,1)S(1)} %get-tuple-element.24), channel_id=1, source_target_pairs={{0,1},{1,2},{2,3},{4,5},{5,6},{6,7},{8,9},{9,10},{10,11},{12,13},{... | collective-permute-start | bytes 147464 | tf_op jit(solution)/shard_map/ppermute | solution.py:23
  32.9 3.7 %collective-permute-start.1 = (bf16[1,32,768]{1,2,0:T(8,128)(2,1)S(1)}, bf16[1,32,768]{1,2,0:T(8,128)(2,1)S(1)}, u32[]{:S(2)}, u32[]{:S(2)}) collective-permute-start(bf16[1,32,768]{1,2,0:T(8,128)(2,1)S(1)} %get-tuple-element.25), channel_id=1, source_target_pairs={{1,0},{2,1},{3,2},{5,4},{6,5},{7,6},{9,8},{10,9},{11,10},{13,12},{... | collective-permute-start | bytes 147464 | tf_op jit(solution)/shard_map/ppermute | solution.py:26
  34.7 1.9 copy-start.12
  36.6 0.7 copy-start.16
  49.1 0.9 copy-start.3
  49.1 11.1 %copy-start.5 = (f32[4,128,192]{1,2,0:T(8,128)S(1)}, f32[4,128,192]{1,2,0:T(8,128)}, u32[]{:S(2)}) copy-start(f32[4,128,192]{1,2,0:T(8,128)} %copy-done.4) | copy-start | bytes 1179652
  49.1 85.3 %reduce-scatter.6.cloned.1.call-start = ((), (), s32[]{:S(2)}) async-start(), calls=%async_computation.3 | async-start | bytes 3932160 | tf_op jit(solution)/shard_map/reduce_scatter | solution.py:144
  50.0 12.5 %collective-permute-start.2 = (bf16[1,32,768]{2,1,0:T(8,128)(2,1)S(1)}, bf16[1,32,768]{2,1,0:T(8,128)(2,1)S(1)}, u32[]{:S(2)}, u32[]{:S(2)}) collective-permute-start(bf16[1,32,768]{2,1,0:T(8,128)(2,1)S(1)} %get-tuple-element.22), channel_id=1, source_target_pairs={{1,0},{2,1},{3,2},{5,4},{6,5},{7,6},{9,8},{10,9},{11,10},{13,12},{... | collective-permute-start | bytes 147464 | tf_op jit(solution)/shard_map/ppermute | solution.py:26
  51.3 9.0 %collective-permute-start.3 = (bf16[1,32,768]{2,1,0:T(8,128)(2,1)S(1)}, bf16[1,32,768]{2,1,0:T(8,128)(2,1)S(1)}, u32[]{:S(2)}, u32[]{:S(2)}) collective-permute-start(bf16[1,32,768]{2,1,0:T(8,128)(2,1)S(1)} %get-tuple-element.23), channel_id=1, source_target_pairs={{0,1},{1,2},{2,3},{4,5},{5,6},{6,7},{8,9},{9,10},{10,11},{12,13},{... | collective-permute-start | bytes 147464 | tf_op jit(solution)/shard_map/ppermute | solution.py:23
  62.5 2.5 %copy-start.10 = (bf16[1,512,768]{1,2,0:T(8,128)(2,1)S(1)}, bf16[1,512,768]{1,2,0:T(8,128)(2,1)}, u32[]{:S(2)}) copy-start(bf16[1,512,768]{1,2,0:T(8,128)(2,1)} %copy-done.9) | copy-start | bytes 2359300
  64.6 1.7 copy-start.15
  65.3 1.0 copy-start.11
  71.7 2.0 copy-start.7
  79.6 127.8 %reduce-scatter.8.cloned.1.call-start = ((), (), s32[]{:S(2)}) async-start(), calls=%async_computation.4 | async-start | bytes 2654208 | tf_op jit(solution)/shard_map/reduce_scatter | solution.py:171
  98.5 1.8 copy-start.8
  100.3 6.1 %copy-start.1 = (bf16[1,128,768]{1,2,0:T(8,128)(2,1)S(1)}, bf16[1,128,768]{1,2,0:T(8,128)(2,1)}, u32[]{:S(2)}) copy-start(bf16[1,128,768]{1,2,0:T(8,128)(2,1)} %copy-done) | copy-start | bytes 589828
  100.3 6.1 %copy-start.17 = (bf16[1,32,768]{1,2,0:T(8,128)(2,1)S(1)}, bf16[1,32,768]{1,2,0:T(8,128)(2,1)}, u32[]{:S(2)}) copy-start(bf16[1,32,768]{1,2,0:T(8,128)(2,1)} %copy-done.16) | copy-start | bytes 147460
  105.5 2.7 %copy-start.13 = (bf16[1,32,768]{1,2,0:T(8,128)(2,1)S(1)}, bf16[1,32,768]{1,2,0:T(8,128)(2,1)}, u32[]{:S(2)}) copy-start(bf16[1,32,768]{1,2,0:T(8,128)(2,1)} %copy-done.12) | copy-start | bytes 147460
Sparse Core Ops, SparseCore 0:
  49.2 44.4 reduce-scatter.9
  96.4 37.9 reduce-scatter.5
  138.5 68.8 reduce-scatter.7
where the time goes:
time: 215 us; the launch traced here: 214 us
  waiting for transfers between devices  110 us (51%)
  matrix products  29.1 us (14%)
  local copies, waits for them, and re-layouts  23.7 us (11%)
  blocking collectives  19 us (9%)
  between operations  14.1 us (7%)
  starting transfers between devices  11.8 us (5%)
  other arithmetic  5.93 us (3%)
    reduce_scatter x1, waiting for transfers between devices, body(): lax.psum_scatter(partial_value, 'dp', scatter_dimension=0, tiled=True)  71.1 us
    reduce_scatter x1, waiting for transfers between devices, body(): lax.psum_scatter(key_side(grad_scores, soft_rounded, queries[0], grad_att...  23.8 us
    unnamed x44, local copies, waits for them, and re-layouts  18.1 us
    unnamed x4, waiting for transfers between devices  13.9 us
    all_gather x1, blocking collectives, body(): lax.all_gather(key_rows, 'seq', axis=1, tiled=True)  10.3 us
    ppermute x2, starting transfers between devices, padded(): lax.ppermute(lax.slice_in_dim(block, block.shape[dim] - width, None, axis...  8.95 us
    all_gather x1, blocking collectives, body(): lax.all_gather(value_rows, 'seq', axis=1, tiled=True)  8.72 us
    dot_general x3, matrix products, body(): jnp.einsum('pc,dc->pd', reverse_rows, conv_weight[:, kernel_tap_index, :]...  6.41 us
  transfers between devices with their start and end apart: 7, of which 4 were waited for; matrix products, arithmetic and copies ran while one was open for 19% of the time, Pallas kernels for 0%

commit v1 on v0

v1 whole, which is shorter than its diff:
```python
import functools
import math

import jax
import jax.numpy as jnp
from jax import lax
from jax.experimental import pallas as pl
from jax.experimental.pallas import tpu as pltpu
from jax.sharding import PartitionSpec as P

HEAD_DIM = 192
WIN = 256
TAPS = 3
STEP = 32
N = 4
F32 = jnp.float32
BF16 = jnp.bfloat16
MESH = pl.DeviceIdType.MESH

tanh_scale = 0.7978845608028654
cubic_term = 0.044715
norm_epsilon = 1e-06


def gelu_pair(value):
    square = value * value
    inner = tanh_scale * (value + cubic_term * value * square)
    tangent = jnp.tanh(inner)
    half = 0.5 * (1.0 + tangent)
    result = value * half
    slope = half + 0.5 * value * (1.0 - tangent * tangent) * tanh_scale * (
        1.0 + 3.0 * cubic_term * square
    )
    return (result, slope)


def window_start(head):
    return pl.multiple_of(384 * (head // 2) + 128 * (head % 2), 128)


def nt(a, b):
    return lax.dot_general(a, b, (((1,), (1,)), ((), ())), preferred_element_type=F32)


def tn(a, b):
    return lax.dot_general(a, b, (((0,), (0,)), ((), ())), preferred_element_type=F32)


def nn(a, b):
    return lax.dot_general(a, b, (((1,), (0,)), ((), ())), preferred_element_type=F32)


def merge(even, odd):
    return jnp.concatenate(
        [even[:, :128], even[:, 128:] + odd[:, :128], odd[:, 128:]], axis=1
    )


def as_row(column):
    wide = jnp.broadcast_to(column, (column.shape[0], 128))
    return wide.T[:8]


def as_column(row):
    return jnp.broadcast_to(row, (128, 128)).T


def kernel(
    q_ref, k_ref, v_ref, g_ref, w_hbm,
    conv_ref, dq_ref, dk_ref, dv_ref, gw_ref,
    w_ref, qkv, gh, ga, gab, gg, soft, att, normed, gn, act, stat, dqkv, land,
    w_sem, send_sem, recv_sem,
):
    me = lax.axis_index("seq")
    rows, feats = q_ref.shape
    total = rows * N
    inverse = 1.0 / math.sqrt(HEAD_DIM)
    half_lanes = pl.multiple_of(384 * (me // 2), 128)
    my_start = window_start(me)
    my_rows = pl.multiple_of(rows * me, rows)
    sends = []

    def peer_of(o):
        return lax.rem(me + o, N)

    def rdma(phase, o, src, dst, when=None):
        copy = pltpu.make_async_remote_copy(
            src_ref=src, dst_ref=dst,
            send_sem=send_sem.at[phase, o], recv_sem=recv_sem.at[phase, o],
            device_id={"seq": peer_of(o)}, device_id_type=MESH,
        )
        return copy

    loads = [pltpu.make_async_copy(w_hbm.at[t], w_ref.at[t], w_sem.at[t]) for t in range(TAPS)]
    for load in loads:
        load.start()

    barrier = pltpu.get_barrier_semaphore()
    for o in (1, 2, 3):
        pl.semaphore_signal(barrier, inc=1, device_id={"seq": peer_of(o)}, device_id_type=MESH)
    pl.semaphore_wait(barrier, 3)

    has_next, has_prev = me < N - 1, me > 0
    down = pltpu.make_async_remote_copy(
        src_ref=g_ref.at[pl.ds(rows - STEP, STEP)], dst_ref=gh.at[pl.ds(0, STEP)],
        send_sem=send_sem.at[0, 0], recv_sem=recv_sem.at[0, 0],
        device_id={"seq": lax.rem(me + 1, N)}, device_id_type=MESH,
    )
    up = pltpu.make_async_remote_copy(
        src_ref=g_ref.at[pl.ds(0, STEP)], dst_ref=gh.at[pl.ds(rows + STEP, STEP)],
        send_sem=send_sem.at[1, 0], recv_sem=recv_sem.at[1, 0],
        device_id={"seq": lax.rem(me + N - 1, N)}, device_id_type=MESH,
    )
    pl.when(has_next)(lambda: down.start())
    pl.when(has_prev)(lambda: up.start())

    first = []
    for o in (2, 3, 1):
        start = window_start(peer_of(o))
        for i, ref in enumerate((q_ref, k_ref, v_ref)):
            copy = rdma(i, o, ref.at[:, pl.ds(start, WIN)], qkv.at[i, pl.ds(my_rows, rows)])
            copy.start()
            first.append(copy)
    grads = []
    for o in (2, 3, 1):
        lanes = pl.multiple_of(384 * (peer_of(o) // 2), 128)
        copy = rdma(
            3, o, g_ref.at[:, pl.ds(lanes, 384)],
            gg.at[pl.ds(pl.multiple_of(STEP + rows * me, STEP), rows)],
        )
        copy.start()
        grads.append(copy)

    for i, ref in enumerate((q_ref, k_ref, v_ref)):
        qkv[i, pl.ds(my_rows, rows)] = ref[:, pl.ds(my_start, WIN)]
    gg[pl.ds(0, STEP)] = jnp.zeros((STEP, 384), BF16)
    gg[pl.ds(STEP + total, STEP)] = jnp.zeros((STEP, 384), BF16)
    gg[pl.ds(pl.multiple_of(STEP + rows * me, STEP), rows)] = g_ref[:, pl.ds(half_lanes, 384)]
    gh[pl.ds(STEP, rows)] = g_ref[...]

    @pl.when(me == 0)
    def _():
        gh[pl.ds(0, STEP)] = jnp.zeros((STEP, feats), BF16)

    @pl.when(me == N - 1)
    def _():
        gh[pl.ds(rows + STEP, STEP)] = jnp.zeros((STEP, feats), BF16)

    pl.when(has_prev)(lambda: down.wait_recv())
    pl.when(has_next)(lambda: up.wait_recv())
    for load in loads:
        load.wait()

    acc = nt(gh[pl.ds(2 * STEP, rows)], w_ref[0])
    acc += nt(gh[pl.ds(STEP, rows)], w_ref[1])
    acc += nt(gh[pl.ds(0, rows)], w_ref[2])
    ga[...] = acc.astype(BF16)
    spread = []
    for o in (2, 3, 1):
        copy = rdma(
            4, o, ga.at[:, pl.ds(window_start(peer_of(o)), WIN)], gab.at[pl.ds(my_rows, rows)]
        )
        copy.start()
        spread.append(copy)
    gab[pl.ds(my_rows, rows)] = ga[:, pl.ds(my_start, WIN)]

    lane = lax.broadcasted_iota(jnp.int32, (rows, WIN), 1)
    low = 64 * (me % 2)
    mask32 = jnp.logical_and(lane >= low, lane < low + HEAD_DIM).astype(F32)
    mask = mask32.astype(BF16)

    for copy in first:
        copy.wait_recv()
    for i in range(3):
        for b in range(N):
            part = pl.ds(b * rows, rows)
            qkv[i, part] = qkv[i, part] * mask

    keys, values = qkv[1], qkv[2]
    for b in range(N):
        part = pl.ds(b * rows, rows)
        scores = nt(qkv[0, part], keys)
        top = jnp.max(scores, axis=-1, keepdims=True)
        expo = jnp.exp((scores - top) * inverse)
        prob = expo * (1.0 / jnp.sum(expo, axis=-1, keepdims=True))
        soft[part] = prob
        out = nn(prob.astype(BF16), values).astype(BF16)
        att[part] = out
        wide = out.astype(F32)
        stat[0, me, :, b * rows : (b + 1) * rows] = as_row(
            jnp.sum(wide * wide, axis=-1, keepdims=True)
        )
    stats = []
    for o in (2, 3, 1):
        copy = rdma(5, o, stat.at[0, me], stat.at[0, me])
        copy.start()
        stats.append(copy)
    for copy in spread:
        copy.wait_recv()
    for copy in stats:
        copy.wait_recv()

    act[me, pl.ds(0, STEP)] = jnp.zeros((STEP, WIN), BF16)
    act[me, pl.ds(STEP + total, STEP)] = jnp.zeros((STEP, WIN), BF16)

    def factor(b):
        lanes = slice(b * rows, (b + 1) * rows)
        mean = (
            stat[0, 0, :1, lanes] + stat[0, 1, :1, lanes]
            + stat[0, 2, :1, lanes] + stat[0, 3, :1, lanes]
        ) * (1.0 / feats)
        one = as_column(lax.rsqrt(mean + norm_epsilon))
        return jnp.concatenate([one, one], axis=1)

    for b in range(N):
        part = pl.ds(b * rows, rows)
        x = att[part].astype(F32) * factor(b)
        value, slope = gelu_pair(x)
        act[me, pl.ds(STEP + b * rows, rows)] = value.astype(BF16)
        grad = gab[part].astype(F32) * slope * mask32
        normed[part] = x
        gn[part] = grad
        stat[1, me, :, b * rows : (b + 1) * rows] = as_row(
            jnp.sum(grad * x, axis=-1, keepdims=True)
        )
    inner = []
    for o in (2, 3, 1):
        copy = rdma(6, o, stat.at[1, me], stat.at[1, me])
        copy.start()
        inner.append(copy)

    acts = []
    for o in (2, 3, 1):
        peer = peer_of(o)
        some = pl.ds(pl.multiple_of(rows * peer, rows), rows + 2 * STEP)
        full = rdma(7, o, act.at[me], act.at[me])
        piece = rdma(7, o, act.at[me, some], act.at[me, some])
        needs = peer % 2 == me // 2
        pl.when(needs)(lambda full=full: full.start())
        pl.when(jnp.logical_not(needs))(lambda piece=piece: piece.start())
        acts.append((o, needs, full, piece))

    for copy in inner:
        copy.wait_recv()

    queries = qkv[0]
    for b in range(N):
        part = pl.ds(b * rows, rows)
        lanes = slice(b * rows, (b + 1) * rows)
        mean = (
            stat[1, 0, :1, lanes] + stat[1, 1, :1, lanes]
            + stat[1, 2, :1, lanes] + stat[1, 3, :1, lanes]
        ) * (1.0 / feats)
        one = as_column(mean)
        mean = jnp.concatenate([one, one], axis=1)
        grad = (factor(b) * (gn[part] - normed[part] * mean)).astype(BF16)
        att[part] = grad
        prob = soft[part]
        gs = nt(grad, values)
        row_inner = jnp.sum(gs * prob, axis=-1, keepdims=True)
        ds = (prob * (gs - row_inner) * inverse).astype(BF16)
        dqkv[0, part] = nn(ds, keys).astype(BF16)
        pieces = (tn(ds, queries[b * rows : (b + 1) * rows]), tn(prob.astype(BF16), grad))
        sums = pieces if b == 0 else (sums[0] + pieces[0], sums[1] + pieces[1])
    dqkv[1] = sums[0].astype(BF16)
    dqkv[2] = sums[1].astype(BF16)

    back = []
    for o in (2, 3, 1):
        there = pl.ds(pl.multiple_of(rows * peer_of(o), rows), rows)
        for i in range(3):
            copy = rdma(8 + i, o, dqkv.at[i, there], land.at[me, i])
            copy.start()
            back.append(copy)
    for i in range(3):
        land[me, i] = dqkv[i, pl.ds(my_rows, rows)]

    def act_wait_recv(o, method):
        source = lax.rem(me + N - o, N)
        some = pl.ds(my_rows, rows + 2 * STEP)
        full = rdma(7, o, act.at[source], act.at[source])
        piece = rdma(7, o, act.at[source, some], act.at[source, some])
        needs = me % 2 == source // 2
        pl.when(needs)(lambda: full.wait_recv())
        pl.when(jnp.logical_not(needs))(lambda: piece.wait_recv())

    for o in (2, 3, 1):
        act_wait_recv(o, None)
    for copy in grads:
        copy.wait_recv()

    pair = 2 * (me % 2)
    whole = pl.ds(STEP, total)
    mine = merge(act[pair, whole], act[pair + 1, whole])
    mine = mine.T
    scale = 1.0 / math.sqrt(total * lax.axis_size("dp"))
    for t in range(TAPS):
        term = nn(mine, gg[pl.ds((2 - t) * STEP, total)])
        gw_ref[t] = (term * scale).astype(gw_ref.dtype)

    near = pl.ds(my_rows, rows + 2 * STEP)
    nearby = jnp.concatenate(
        [merge(act[0, near], act[1, near]), merge(act[2, near], act[3, near])], axis=1
    )
    out = nn(nearby[:rows], w_ref[0])
    out += nn(nearby[STEP : STEP + rows], w_ref[1])
    out += nn(nearby[2 * STEP :], w_ref[2])
    conv_ref[...] = out.astype(BF16)

    for copy in back:
        copy.wait_recv()
    for i, ref in enumerate((dq_ref, dk_ref, dv_ref)):
        ref[...] = jnp.concatenate(
            [merge(land[0, i], land[1, i]), merge(land[2, i], land[3, i])], axis=1
        )

    pl.when(has_next)(lambda: down.wait_send())
    pl.when(has_prev)(lambda: up.wait_send())
    for copy in first + grads + spread + stats + inner + back:
        copy.wait_send()
    for o, needs, full, piece in acts:
        pl.when(needs)(lambda full=full: full.wait_send())
        pl.when(jnp.logical_not(needs))(lambda piece=piece: piece.wait_send())


def body(queries, key_rows, value_rows, conv_weight, output_gradient):
    rows, feats = queries.shape[1:]
    total = rows * N
    vmem = pl.BlockSpec(memory_space=pltpu.VMEM)
    anyspace = pl.BlockSpec(memory_space=pl.ANY)
    shape = jax.ShapeDtypeStruct
    conv, dq, dk, dv, gw = pl.pallas_call(
        kernel,
        out_shape=[shape((rows, feats), BF16)] * 4 + [shape((TAPS, 384, 384), F32)],
        in_specs=[vmem] * 4 + [anyspace],
        out_specs=[vmem] * 5,
        scratch_shapes=[
            pltpu.VMEM((TAPS, feats, feats), BF16),
            pltpu.VMEM((3, total, WIN), BF16),
            pltpu.VMEM((rows + 2 * STEP, feats), BF16),
            pltpu.VMEM((rows, feats), BF16),
            pltpu.VMEM((total, WIN), BF16),
            pltpu.VMEM((total + 2 * STEP, 384), BF16),
            pltpu.VMEM((total, total), F32),
            pltpu.VMEM((total, WIN), BF16),
            pltpu.VMEM((total, WIN), F32),
            pltpu.VMEM((total, WIN), F32),
            pltpu.VMEM((N, total + 2 * STEP, WIN), BF16),
            pltpu.VMEM((2, N, 8, total), F32),
            pltpu.VMEM((3, total, WIN), BF16),
            pltpu.VMEM((N, 3, rows, WIN), BF16),
            pltpu.SemaphoreType.DMA((TAPS,)),
            pltpu.SemaphoreType.DMA((11, N)),
            pltpu.SemaphoreType.DMA((11, N)),
        ],
        compiler_params=pltpu.CompilerParams(
            collective_id=0, has_side_effects=True, vmem_limit_bytes=48 * 1024 * 1024
        ),
    )(
        queries[0], key_rows[0], value_rows[0], output_gradient[0],
        jnp.transpose(conv_weight, (1, 0, 2)),
    )
    pieces = lax.all_to_all(
        gw.astype(BF16), "seq", split_axis=2, concat_axis=1, tiled=True,
        axis_index_groups=[[0, 1], [2, 3]],
    )
    grad_weight = lax.psum_scatter(pieces.astype(F32), "dp", scatter_dimension=1, tiled=True)
    grad_weight = jnp.transpose(grad_weight, (1, 0, 2))
    return (conv[None], dq[None], dk[None], dv[None], grad_weight)


def solution(mesh):
    row_spec = P("dp", "seq", None)
    return jax.shard_map(
        body,
        mesh=mesh,
        in_specs=(row_spec, row_spec, row_spec, P(), row_spec),
        out_specs=(row_spec, row_spec, row_spec, row_spec, P("dp", None, "seq")),
        check_vma=False,
    )
```

time: 215 us -> 146 us (0.68)
  waiting for transfers between devices: 110 us -> 67.3 us
  Pallas kernels: 0 us -> 42.1 us
  matrix products: 29.1 us -> 0 us
  blocking collectives: 19 us -> 4.68 us
  starting transfers between devices: 11.8 us -> 0.04 us
  local copies, waits for them, and re-layouts: 23.7 us -> 16.7 us
  other arithmetic: 5.93 us -> 0.22 us
    reduce_scatter x2 -> x0, waiting for transfers between devices: 94.9 us -> none  [the longest x1 71.1 us: body(): lax.psum_scatter(partial_value, 'dp', scatter_dimension=0, tiled=True)]
    unnamed x4 -> x2, waiting for transfers between devices: 13.9 us -> 67.3 us
    pallas_call x0 -> x1, Pallas kernels: none -> 42.1 us  [body(): pl.pallas_call(kernel, out_shape=[shape((rows, feats), BF16)] * 4 + [shap...]
    dot_general x14 -> x0, matrix products: 27.6 us -> none  [the longest x3 6.41 us: body(): jnp.einsum('pc,dc->pd', reverse_rows, conv_weight[:, kernel_tap_index, :]...]
    all_gather x2 -> x0, blocking collectives: 19 us -> none  [the longest x1 10.3 us: body(): lax.all_gather(key_rows, 'seq', axis=1, tiled=True)]
    ppermute x4 -> x0, starting transfers between devices: 11.5 us -> none  [the longest x2 8.95 us: padded(): lax.ppermute(lax.slice_in_dim(block, block.shape[dim] - width, None, axis...]
    all_to_all x0 -> x1, blocking collectives: none -> 4.68 us  [body(): lax.all_to_all(gw.astype(BF16), 'seq', split_axis=2, concat_axis=1, tiled...]
    reshape x2 -> x0, local copies, waits for them, and re-layouts: 3.83 us -> none  [the longest x1 1.96 us: key_side(): grad_keys.reshape(row_total, features)]
  transfers between devices with their start and end apart: 7 -> 1, of which waited for: 4 -> 1; matrix products, arithmetic and copies ran while one was open for 19% -> 0% of each run, Pallas kernels for 0% -> 0%
where the time goes in v1:
time: 146 us; the launch traced here: 145 us
  waiting for transfers between devices  67.3 us (46%)
  Pallas kernels  42.1 us (29%)
  local copies, waits for them, and re-layouts  16.7 us (11%)
  between operations  14.1 us (10%)
  blocking collectives  4.68 us (3%)
    unnamed x2, waiting for transfers between devices  67.3 us
    pallas_call x1, Pallas kernels, body(): pl.pallas_call(kernel, out_shape=[shape((rows, feats), BF16)] * 4 + [shap...  42.1 us
    unnamed x15, local copies, waits for them, and re-layouts  14.9 us
    all_to_all x1, blocking collectives, body(): lax.all_to_all(gw.astype(BF16), 'seq', split_axis=2, concat_axis=1, tiled...  4.68 us
  transfers between devices with their start and end apart: 1, of which 1 were waited for; matrix products, arithmetic and copies ran while one was open for 0% of the time, Pallas kernels for 0%

profile of v1, /device:TPU:0, one launch (start us, length us, event | category | flops | bytes accessed | tf_op | source)
XLA Modules:
  0.0 145.2 jit_solution(2103334572304759419)
XLA Ops:
  7.2 0.0 reduce-scatter.4.cloned.1.call-start
  7.2 0.0 copy-start
  7.2 0.9 copy-done
  8.1 0.0 copy-start.1
  8.1 0.9 copy-done.1
  9.1 0.0 copy-start.2
  9.1 0.9 copy-done.2
  10.0 0.0 copy-start.3
  10.0 0.9 copy-done.3
  10.9 42.1 %shard_map.92 = (bf16[128,768]{1,0:T(8,128)(2,1)S(1)}, bf16[128,768]{1,0:T(8,128)(2,1)S(1)}, bf16[128,768]{1,0:T(8,128)(2,1)S(1)}, bf16[128,768]{1,0:T(8,128)(2,1)S(1)}, f32[3,384,384]{2,1,0:T(8,128)S(1)}) custom-call(bf16[128,768]{1,0:T(8,128)(2,1)S(1)} %bitcast.22, bf16[128,768]{1,0:T(8,128)(2,1)S(1)} %bitcast.23, bf16[128,768]{1,0:T(8,128)(2,1)S(1)} %bitcast.24, ...), custom_call_target="tpu_custom_call" | custom-call | tf_op jit(solution)/shard_map/pallas_call | solution.py:332
  53.0 0.1 convert_element_type.15
  53.1 1.0 copy.15
  54.1 4.7 %all_to_all.4 = bf16[3,384,384]{1,0,2:T(4,128)(2,1)S(1)} all-to-all(bf16[3,384,384]{1,0,2:T(4,128)(2,1)S(1)} %copy.15), channel_id=1, replica_groups={{0,1},{2,3},{4,5},{6,7},{8,9},{10,11},{12,13},{14,15},{16,17},{18,19},{..., dimensions={2} | all-to-all | bytes 1769472 | tf_op jit(solution)/shard_map/all_to_all | solution.py:363
  58.8 0.1 copy.16
  58.9 0.1 convert_bitcast_fusion
  59.0 2.7 %copy.21 = f32[3,2,384,192]{3,0,2,1:T(4,128)} copy(f32[3,2,384,192]{2,3,1,0:T(8,128)S(1)} %convert_bitcast_fusion) | data formatting | bytes 3538944
  61.8 4.7 %reshape.16 = f32[768,576]{1,0:T(8,128)} reshape(f32[768,3,192]{2,1,0:T(4,128)} %bitcast.30) | data formatting | bytes 3538944
  66.4 0.0 reduce-scatter.4.cloned.1.call-update
  66.4 67.3 %reduce-scatter.4.cloned.1.call-done = f32[96,576]{1,0:T(8,128)} async-done(((f32[768,576]{1,0:T(8,128)}), f32[96,576]{1,0:T(8,128)}) %reduce-scatter.4.cloned.1.call-update) | async-done | bytes 221200
  133.7 1.1 reshape.17
  134.8 0.8 copy.25
  135.6 0.7 copy.30
  136.3 0.7 copy.31
  137.0 0.7 copy.32
  137.6 0.7 copy.33
Async XLA Ops:
  7.2 126.5 %reduce-scatter.4.cloned.1.call-start = ((), (), s32[]{:S(2)}) async-start(), calls=%async_computation.2 | async-start | bytes 2211840
  7.2 0.9 copy-start
  8.1 0.9 copy-start.1
  9.1 0.9 copy-start.2
  10.0 0.9 copy-start.3
Sparse Core Ops, SparseCore 0:
  66.6 67.1 reduce-scatter.3

commit v2 on v1

--- a/solution.py
+++ b/solution.py
@@ -69,10 +69,12 @@
     q_ref, k_ref, v_ref, g_ref, w_hbm,
     conv_ref, dq_ref, dk_ref, dv_ref, gw_ref,
     w_ref, qkv, gh, ga, gab, gg, soft, att, normed, gn, act, stat, dqkv, land,
-    w_sem, send_sem, recv_sem,
+    w_sem, send_sem, recv_sem, *tail,
 ):
     me = lax.axis_index("seq")
     rows, feats = q_ref.shape
+    ring = lax.axis_index("dp")
+    tx, tz, core = ring % 2, ring // 2, me % 2
     total = rows * N
     inverse = 1.0 / math.sqrt(HEAD_DIM)
     half_lanes = pl.multiple_of(384 * (me // 2), 128)
@@ -92,13 +94,27 @@
         return copy
 
     loads = [pltpu.make_async_copy(w_hbm.at[t], w_ref.at[t], w_sem.at[t]) for t in range(TAPS)]
-    for load in loads:
+    grad_rows = pl.ds(pl.multiple_of(STEP + rows * me, STEP), rows)
+    g_loads = [
+        pltpu.make_async_copy(g_ref, gh.at[pl.ds(STEP, rows)], w_sem.at[TAPS]),
+        pltpu.make_async_copy(g_ref.at[:, pl.ds(half_lanes, 384)], gg.at[grad_rows], w_sem.at[TAPS + 1]),
+    ]
+    own = [
+        pltpu.make_async_copy(
+            ref.at[:, pl.ds(my_start, WIN)], qkv.at[i, pl.ds(my_rows, rows)], w_sem.at[TAPS + 2 + i]
+        )
+        for i, ref in enumerate((q_ref, k_ref, v_ref))
+    ]
+    for load in g_loads + loads + own:
         load.start()
 
     barrier = pltpu.get_barrier_semaphore()
     for o in (1, 2, 3):
         pl.semaphore_signal(barrier, inc=1, device_id={"seq": peer_of(o)}, device_id_type=MESH)
-    pl.semaphore_wait(barrier, 3)
+    if tail:
+        for other in [ring + 1 - 2 * tx] + [2 * lax.rem(tz + o, 4) + tx for o in (1, 2, 3)]:
+            pl.semaphore_signal(barrier, inc=1, device_id={"dp": other}, device_id_type=MESH)
+    pl.semaphore_wait(barrier, 7 if tail else 3)
 
     has_next, has_prev = me < N - 1, me > 0
     down = pltpu.make_async_remote_copy(
@@ -125,18 +141,13 @@
     for o in (2, 3, 1):
         lanes = pl.multiple_of(384 * (peer_of(o) // 2), 128)
         copy = rdma(
-            3, o, g_ref.at[:, pl.ds(lanes, 384)],
-            gg.at[pl.ds(pl.multiple_of(STEP + rows * me, STEP), rows)],
+            3, o, g_ref.at[:, pl.ds(lanes, 384)], gg.at[grad_rows]
         )
         copy.start()
         grads.append(copy)
 
-    for i, ref in enumerate((q_ref, k_ref, v_ref)):
-        qkv[i, pl.ds(my_rows, rows)] = ref[:, pl.ds(my_start, WIN)]
     gg[pl.ds(0, STEP)] = jnp.zeros((STEP, 384), BF16)
     gg[pl.ds(STEP + total, STEP)] = jnp.zeros((STEP, 384), BF16)
-    gg[pl.ds(pl.multiple_of(STEP + rows * me, STEP), rows)] = g_ref[:, pl.ds(half_lanes, 384)]
-    gh[pl.ds(STEP, rows)] = g_ref[...]
 
     @pl.when(me == 0)
     def _():
@@ -148,7 +159,7 @@
 
     pl.when(has_prev)(lambda: down.wait_recv())
     pl.when(has_next)(lambda: up.wait_recv())
-    for load in loads:
+    for load in g_loads + loads:
         load.wait()
 
     acc = nt(gh[pl.ds(2 * STEP, rows)], w_ref[0])
@@ -169,6 +180,8 @@
     mask32 = jnp.logical_and(lane >= low, lane < low + HEAD_DIM).astype(F32)
     mask = mask32.astype(BF16)
 
+    for load in own:
+        load.wait()
     for copy in first:
         copy.wait_recv()
     for i in range(3):
@@ -293,10 +306,26 @@
     whole = pl.ds(STEP, total)
     mine = merge(act[pair, whole], act[pair + 1, whole])
     mine = mine.T
+    crossing = []
     scale = 1.0 / math.sqrt(total * lax.axis_size("dp"))
     for t in range(TAPS):
         term = nn(mine, gg[pl.ds((2 - t) * STEP, total)])
-        gw_ref[t] = (term * scale).astype(gw_ref.dtype)
+        term = term * scale
+        if not tail:
+            gw_ref[t] = term
+            continue
+        gwf, xs, xr, zs, zo, zr, fin, x_send, x_recv, z_send, z_recv, c_sem = tail
+        gwf[t] = term
+        xs[t] = term.astype(BF16)
+        for j in range(2):
+            there = pl.ds(pl.multiple_of(96 * (2 * j + 1 - tx), 96), 96)
+            copy = pltpu.make_async_remote_copy(
+                src_ref=xs.at[t, there], dst_ref=xr.at[t, j],
+                send_sem=x_send.at[t, j], recv_sem=x_recv.at[t, j],
+                device_id={"dp": ring + 1 - 2 * tx}, device_id_type=MESH,
+            )
+            copy.start()
+            crossing.append(copy)
 
     near = pl.ds(my_rows, rows + 2 * STEP)
     nearby = jnp.concatenate(
@@ -306,6 +335,24 @@
     out += nn(nearby[STEP : STEP + rows], w_ref[1])
     out += nn(nearby[2 * STEP :], w_ref[2])
     conv_ref[...] = out.astype(BF16)
+
+    along = []
+    if tail:
+        for t in range(TAPS):
+            for j in range(2):
+                crossing[2 * t + j].wait_recv()
+                here = pl.ds(pl.multiple_of(96 * (2 * j + tx), 96), 96)
+                block = gwf[t, here] + xr[t, j].astype(F32)
+                zs[j, t] = block
+                zo[j, t] = block.astype(BF16)
+                target = 2 * core + j
+                copy = pltpu.make_async_remote_copy(
+                    src_ref=zo.at[j, t], dst_ref=zr.at[tz, t],
+                    send_sem=z_send.at[t, j], recv_sem=z_recv.at[t, tz],
+                    device_id={"dp": 2 * target + tx}, device_id_type=MESH,
+                )
+                pl.when(target != tz)(lambda copy=copy: copy.start())
+                along.append((target != tz, copy))
 
     for copy in back:
         copy.wait_recv()
@@ -314,13 +361,74 @@
             [merge(land[0, i], land[1, i]), merge(land[2, i], land[3, i])], axis=1
         )
 
+    if tail:
+        owner = tz // 2 == core
+        other = 2 * (me // 2) + 1 - core
+        lanes = pl.multiple_of(128 * (1 - core), 128)
+        hand = [
+            pltpu.make_async_remote_copy(
+                src_ref=fin.at[t, :, pl.ds(lanes, WIN)], dst_ref=fin.at[t, :, pl.ds(lanes, WIN)],
+                send_sem=c_sem.at[0, t], recv_sem=c_sem.at[1, t],
+                device_id={"seq": other}, device_id_type=MESH,
+            )
+            for t in range(TAPS)
+        ]
+        mine_lanes = pl.multiple_of(128 * core, 128)
+        take = [
+            pltpu.make_async_remote_copy(
+                src_ref=fin.at[t, :, pl.ds(mine_lanes, WIN)],
+                dst_ref=fin.at[t, :, pl.ds(mine_lanes, WIN)],
+                send_sem=c_sem.at[0, t], recv_sem=c_sem.at[1, t],
+                device_id={"seq": other}, device_id_type=MESH,
+            )
+            for t in range(TAPS)
+        ]
+
+        @pl.when(owner)
+        def _():
+            for t in range(TAPS):
+                fin[t] = zs[tz % 2, t]
+                for o in (1, 2, 3):
+                    source = lax.rem(tz + o, 4)
+                    pltpu.make_async_remote_copy(
+                        src_ref=zo.at[0, t], dst_ref=zr.at[source, t],
+                        send_sem=z_send.at[t, 0], recv_sem=z_recv.at[t, source],
+                        device_id={"dp": 2 * source + tx}, device_id_type=MESH,
+                    ).wait_recv()
+                    fin[t] += zr[source, t].astype(F32)
+                hand[t].start()
+            for copy in hand:
+                copy.wait_send()
+
+        @pl.when(jnp.logical_not(owner))
+        def _():
+            for copy in take:
+                copy.wait_recv()
+
+        for t in range(TAPS):
+            both = fin[t, :, pl.ds(mine_lanes, WIN)]
+            gw_ref[t] = jnp.where(core == 0, both[:, :HEAD_DIM], both[:, WIN - HEAD_DIM :])
+        for go, copy in along:
+            pl.when(go)(lambda copy=copy: copy.wait_send())
+
     pl.when(has_next)(lambda: down.wait_send())
     pl.when(has_prev)(lambda: up.wait_send())
-    for copy in first + grads + spread + stats + inner + back:
+    for copy in first + grads + spread + stats + inner + back + crossing:
         copy.wait_send()
     for o, needs, full, piece in acts:
         pl.when(needs)(lambda full=full: full.wait_send())
         pl.when(jnp.logical_not(needs))(lambda piece=piece: piece.wait_send())
+
+
+def store_kernel(*refs):
+    count = (len(refs) - 1) // 2
+    copies = [
+        pltpu.make_async_copy(refs[i], refs[count + i], refs[-1].at[i]) for i in range(count)
+    ]
+    for copy in copies:
+        copy.start()
+    for copy in copies:
+        copy.wait()
 
 
 def body(queries, key_rows, value_rows, conv_weight, output_gradient):
@@ -329,10 +437,26 @@
     vmem = pl.BlockSpec(memory_space=pltpu.VMEM)
     anyspace = pl.BlockSpec(memory_space=pl.ANY)
     shape = jax.ShapeDtypeStruct
-    conv, dq, dk, dv, gw = pl.pallas_call(
+    inside = lax.axis_size("dp") == 8
+    gw_shape = (TAPS, 96, HEAD_DIM) if inside else (TAPS, 384, 384)
+    tail = [
+        pltpu.VMEM((TAPS, 384, 384), F32),
+        pltpu.VMEM((TAPS, 384, 384), BF16),
+        pltpu.VMEM((TAPS, 2, 96, 384), BF16),
+        pltpu.VMEM((2, TAPS, 96, 384), F32),
+        pltpu.VMEM((2, TAPS, 96, 384), BF16),
+        pltpu.VMEM((4, TAPS, 96, 384), BF16),
+        pltpu.VMEM((TAPS, 96, 384), F32),
+        pltpu.SemaphoreType.DMA((TAPS, 2)),
+        pltpu.SemaphoreType.DMA((TAPS, 2)),
+        pltpu.SemaphoreType.DMA((TAPS, 2)),
+        pltpu.SemaphoreType.DMA((TAPS, 4)),
+        pltpu.SemaphoreType.DMA((2, TAPS)),
+    ]
+    outs = pl.pallas_call(
         kernel,
-        out_shape=[shape((rows, feats), BF16)] * 4 + [shape((TAPS, 384, 384), F32)],
-        in_specs=[vmem] * 4 + [anyspace],
+        out_shape=[shape((rows, feats), BF16)] * 4 + [shape(gw_shape, F32)],
+        in_specs=[pl.BlockSpec(memory_space=pltpu.HBM)] * 5,
         out_specs=[vmem] * 5,
         scratch_shapes=[
             pltpu.VMEM((TAPS, feats, feats), BF16),
@@ -349,24 +473,34 @@
             pltpu.VMEM((2, N, 8, total), F32),
             pltpu.VMEM((3, total, WIN), BF16),
             pltpu.VMEM((N, 3, rows, WIN), BF16),
-            pltpu.SemaphoreType.DMA((TAPS,)),
+            pltpu.SemaphoreType.DMA((TAPS + 5,)),
             pltpu.SemaphoreType.DMA((11, N)),
             pltpu.SemaphoreType.DMA((11, N)),
-        ],
+        ] + (tail if inside else []),
         compiler_params=pltpu.CompilerParams(
-            collective_id=0, has_side_effects=True, vmem_limit_bytes=48 * 1024 * 1024
+            collective_id=0, has_side_effects=True, vmem_limit_bytes=int(62.5 * 2**20)
         ),
     )(
         queries[0], key_rows[0], value_rows[0], output_gradient[0],
         jnp.transpose(conv_weight, (1, 0, 2)),
     )
-    pieces = lax.all_to_all(
-        gw.astype(BF16), "seq", split_axis=2, concat_axis=1, tiled=True,
-        axis_index_groups=[[0, 1], [2, 3]],
-    )
-    grad_weight = lax.psum_scatter(pieces.astype(F32), "dp", scatter_dimension=1, tiled=True)
-    grad_weight = jnp.transpose(grad_weight, (1, 0, 2))
-    return (conv[None], dq[None], dk[None], dv[None], grad_weight)
+    if not inside:
+        pieces = lax.all_to_all(
+            outs[4].astype(BF16), "seq", split_axis=2, concat_axis=1, tiled=True,
+            axis_index_groups=[[0, 1], [2, 3]],
+        )
+        gw = lax.psum_scatter(pieces.astype(F32), "dp", scatter_dimension=1, tiled=True)
+        outs = [*outs[:4], gw]
+    else:
+        outs = pl.pallas_call(
+            store_kernel,
+            out_shape=[shape(out.shape, out.dtype) for out in outs],
+            in_specs=[anyspace] * 5,
+            out_specs=[pl.BlockSpec(memory_space=pltpu.HBM)] * 5,
+            scratch_shapes=[pltpu.SemaphoreType.DMA((5,))],
+            compiler_params=pltpu.CompilerParams(vmem_limit_bytes=int(62.5 * 2**20)),
+        )(*outs)
+    return (*(out[None] for out in outs[:4]), jnp.transpose(outs[4], (1, 0, 2)))
 
 
 def solution(mesh):

time: 146 us -> 88.9 us (0.61)
  waiting for transfers between devices: 67.3 us -> 0 us
  Pallas kernels: 42.1 us -> 88.1 us
  local copies, waits for them, and re-layouts: 16.7 us -> 0 us
  between operations: 14.1 us -> 0.64 us
  blocking collectives: 4.68 us -> 0 us
    unnamed x2 -> x0, waiting for transfers between devices: 67.3 us -> none
    pallas_call x0 -> x1, Pallas kernels: none -> 33.9 us  [body(): pl.pallas_call(store_kernel, out_shape=[shape(out.shape, out.dtype) for o...]
    unnamed x15 -> x0, local copies, waits for them, and re-layouts: 14.9 us -> none
    pallas_call x1, Pallas kernels: 42.1 us -> 54.2 us  [body(): pl.pallas_call(kernel, out_shape=[shape((rows, feats), BF16)] * 4 + [shap...]
    all_to_all x1 -> x0, blocking collectives: 4.68 us -> none  [body(): lax.all_to_all(gw.astype(BF16), 'seq', split_axis=2, concat_axis=1, tiled...]
  transfers between devices with their start and end apart: 1 -> 0, of which waited for: 1 -> 0; matrix products, arithmetic and copies ran while one was open for 0% -> 0% of each run, Pallas kernels for 0% -> 0%
where the time goes in v2:
time: 88.9 us; the launch traced here: 88.8 us
  Pallas kernels  88.1 us (99%)
    pallas_call x1, Pallas kernels, body(): pl.pallas_call(kernel, out_shape=[shape((rows, feats), BF16)] * 4 + [shap...  54.2 us
    pallas_call x1, Pallas kernels, body(): pl.pallas_call(store_kernel, out_shape=[shape(out.shape, out.dtype) for o...  33.9 us

profile of v2, /device:TPU:0, one launch (start us, length us, event | category | flops | bytes accessed | tf_op | source)
XLA Modules:
  0.0 88.8 jit_solution(1385111825088526328)
XLA Ops:
  0.6 54.2 %shard_map.92 = (bf16[128,768]{1,0:T(8,128)(2,1)}, bf16[128,768]{1,0:T(8,128)(2,1)}, bf16[128,768]{1,0:T(8,128)(2,1)}, bf16[128,768]{1,0:T(8,128)(2,1)}, f32[3,96,192]{2,1,0:T(8,128)}) custom-call(bf16[128,768]{1,0:T(8,128)(2,1)} %bitcast.11, bf16[128,768]{1,0:T(8,128)(2,1)} %bitcast.12, bf16[128,768]{1,0:T(8,128)(2,1)} %bitcast.13, ...), custom_call_target="tpu_custom_call" | custom-call | tf_op jit(solution)/shard_map/pallas_call | solution.py:456
  54.9 33.9 %shard_map.93 = (bf16[128,768]{1,0:T(8,128)(2,1)}, bf16[128,768]{1,0:T(8,128)(2,1)}, bf16[128,768]{1,0:T(8,128)(2,1)}, bf16[128,768]{1,0:T(8,128)(2,1)}, f32[3,96,192]{2,1,0:T(8,128)}) custom-call(bf16[128,768]{1,0:T(8,128)(2,1)} %get-tuple-element.15.refs_0_, bf16[128,768]{1,0:T(8,128)(2,1)} %get-tuple-element.16.refs_1_, ...), custom_call_target="tpu_custom_call" | custom-call | tf_op jit(solution)/shard_map/pallas_call | solution.py:495

commit v3 on v2

--- a/solution.py
+++ b/solution.py
@@ -69,7 +69,7 @@
     q_ref, k_ref, v_ref, g_ref, w_hbm,
     conv_ref, dq_ref, dk_ref, dv_ref, gw_ref,
     w_ref, qkv, gh, ga, gab, gg, soft, att, normed, gn, act, stat, dqkv, land,
-    w_sem, send_sem, recv_sem, *tail,
+    xq, xa, w_sem, send_sem, recv_sem, *tail,
 ):
     me = lax.axis_index("seq")
     rows, feats = q_ref.shape
@@ -82,14 +82,25 @@
     my_rows = pl.multiple_of(rows * me, rows)
     sends = []
 
+    chip = me // 2
+    partner = 2 * chip + 1 - core
+    cross = 2 * (1 - chip) + core
+    diagonal = 2 * (1 - chip) + 1 - core
+    cross_rows = pl.ds(pl.multiple_of(rows * cross, rows), rows)
+    their_rows = pl.ds(pl.multiple_of(rows * partner, rows), rows)
+    their_start = window_start(partner)
+    across_lanes = pl.multiple_of(384 * (1 - chip), 128)
+    mine_in_block = pl.ds(pl.multiple_of(128 * core, 128), WIN)
+    theirs_in_block = pl.ds(pl.multiple_of(128 * (1 - core), 128), WIN)
+
     def peer_of(o):
-        return lax.rem(me + o, N)
-
-    def rdma(phase, o, src, dst, when=None):
+        return (None, partner, cross, diagonal)[o]
+
+    def rdma(phase, o, src, dst, target=None):
         copy = pltpu.make_async_remote_copy(
             src_ref=src, dst_ref=dst,
             send_sem=send_sem.at[phase, o], recv_sem=recv_sem.at[phase, o],
-            device_id={"seq": peer_of(o)}, device_id_type=MESH,
+            device_id={"seq": peer_of(o) if target is None else target}, device_id_type=MESH,
         )
         return copy
 
@@ -130,21 +141,20 @@
     pl.when(has_next)(lambda: down.start())
     pl.when(has_prev)(lambda: up.start())
 
-    first = []
-    for o in (2, 3, 1):
-        start = window_start(peer_of(o))
-        for i, ref in enumerate((q_ref, k_ref, v_ref)):
-            copy = rdma(i, o, ref.at[:, pl.ds(start, WIN)], qkv.at[i, pl.ds(my_rows, rows)])
-            copy.start()
-            first.append(copy)
-    grads = []
-    for o in (2, 3, 1):
-        lanes = pl.multiple_of(384 * (peer_of(o) // 2), 128)
-        copy = rdma(
-            3, o, g_ref.at[:, pl.ds(lanes, 384)], gg.at[grad_rows]
-        )
+    across, first, grads = [], [], []
+    for i, ref in enumerate((q_ref, k_ref, v_ref)):
+        copy = rdma(i, 2, ref.at[:, pl.ds(across_lanes, 384)], xq.at[i])
         copy.start()
-        grads.append(copy)
+        across.append(copy)
+    for i, ref in enumerate((q_ref, k_ref, v_ref)):
+        copy = rdma(i, 1, ref.at[:, pl.ds(their_start, WIN)], qkv.at[i, pl.ds(my_rows, rows)])
+        copy.start()
+        first.append(copy)
+    g_across = rdma(3, 2, g_ref.at[:, pl.ds(across_lanes, 384)], gg.at[grad_rows])
+    g_across.start()
+    g_near = rdma(3, 1, g_ref.at[:, pl.ds(half_lanes, 384)], gg.at[grad_rows])
+    g_near.start()
+    grads = [g_across, g_near]
 
     gg[pl.ds(0, STEP)] = jnp.zeros((STEP, 384), BF16)
     gg[pl.ds(STEP + total, STEP)] = jnp.zeros((STEP, 384), BF16)
@@ -166,13 +176,11 @@
     acc += nt(gh[pl.ds(STEP, rows)], w_ref[1])
     acc += nt(gh[pl.ds(0, rows)], w_ref[2])
     ga[...] = acc.astype(BF16)
-    spread = []
-    for o in (2, 3, 1):
-        copy = rdma(
-            4, o, ga.at[:, pl.ds(window_start(peer_of(o)), WIN)], gab.at[pl.ds(my_rows, rows)]
-        )
-        copy.start()
-        spread.append(copy)
+    ga_across = rdma(4, 2, ga.at[:, pl.ds(across_lanes, 384)], xa)
+    ga_across.start()
+    ga_near = rdma(4, 1, ga.at[:, pl.ds(their_start, WIN)], gab.at[pl.ds(my_rows, rows)])
+    ga_near.start()
+    spread = [ga_across, ga_near]
     gab[pl.ds(my_rows, rows)] = ga[:, pl.ds(my_start, WIN)]
 
     lane = lax.broadcasted_iota(jnp.int32, (rows, WIN), 1)
@@ -180,6 +188,13 @@
     mask32 = jnp.logical_and(lane >= low, lane < low + HEAD_DIM).astype(F32)
     mask = mask32.astype(BF16)
 
+    for i in range(3):
+        across[i].wait_recv()
+        copy = rdma(i, 3, xq.at[i, :, theirs_in_block], qkv.at[i, cross_rows], partner)
+        copy.start()
+        first.append(copy)
+    for i in range(3):
+        qkv[i, cross_rows] = xq[i, :, mine_in_block]
     for load in own:
         load.wait()
     for copy in first:
@@ -208,8 +223,18 @@
         copy = rdma(5, o, stat.at[0, me], stat.at[0, me])
         copy.start()
         stats.append(copy)
-    for copy in spread:
-        copy.wait_recv()
+    ga_across.wait_recv()
+    ga_hop = rdma(4, 3, xa.at[:, theirs_in_block], gab.at[cross_rows], partner)
+    ga_hop.start()
+    gab[cross_rows] = xa[:, mine_in_block]
+    g_across.wait_recv()
+    g_cross = pl.ds(pl.multiple_of(STEP + rows * cross, STEP), rows)
+    g_hop = rdma(3, 3, gg.at[g_cross], gg.at[g_cross], partner)
+    g_hop.start()
+    spread.append(ga_hop)
+    grads.append(g_hop)
+    ga_near.wait_recv()
+    ga_hop.wait_recv()
     for copy in stats:
         copy.wait_recv()
 
@@ -242,16 +267,22 @@
         copy.start()
         inner.append(copy)
 
-    acts = []
-    for o in (2, 3, 1):
-        peer = peer_of(o)
-        some = pl.ds(pl.multiple_of(rows * peer, rows), rows + 2 * STEP)
-        full = rdma(7, o, act.at[me], act.at[me])
-        piece = rdma(7, o, act.at[me, some], act.at[me, some])
-        needs = peer % 2 == me // 2
-        pl.when(needs)(lambda full=full: full.start())
-        pl.when(jnp.logical_not(needs))(lambda piece=piece: piece.start())
-        acts.append((o, needs, full, piece))
+    inside = pl.ds(STEP, total)
+    forms = core == 1 - chip
+    act_across = pltpu.make_async_remote_copy(
+        src_ref=act.at[me, inside], dst_ref=act.at[me, inside],
+        send_sem=send_sem.at[7, 0], recv_sem=recv_sem.at[7, core],
+        device_id={"seq": 2 * (1 - chip) + chip}, device_id_type=MESH,
+    )
+    act_across.start()
+    act_near = rdma(11, 1, act.at[me], act.at[me])
+    act_near.start()
+
+    @pl.when(forms)
+    def _():
+        for i in range(2):
+            act[2 * (1 - chip) + i, pl.ds(0, STEP)] = jnp.zeros((STEP, WIN), BF16)
+            act[2 * (1 - chip) + i, pl.ds(STEP + total, STEP)] = jnp.zeros((STEP, WIN), BF16)
 
     for copy in inner:
         copy.wait_recv()
@@ -288,21 +319,33 @@
     for i in range(3):
         land[me, i] = dqkv[i, pl.ds(my_rows, rows)]
 
-    def act_wait_recv(o, method):
-        source = lax.rem(me + N - o, N)
-        some = pl.ds(my_rows, rows + 2 * STEP)
-        full = rdma(7, o, act.at[source], act.at[source])
-        piece = rdma(7, o, act.at[source, some], act.at[source, some])
-        needs = me % 2 == source // 2
-        pl.when(needs)(lambda: full.wait_recv())
-        pl.when(jnp.logical_not(needs))(lambda: piece.wait_recv())
-
-    for o in (2, 3, 1):
-        act_wait_recv(o, None)
-    for copy in grads:
+    act_near.wait_recv()
+
+    def act_hop(i, row):
+        slot = 2 * (1 - chip) + i
+        some = pl.ds(pl.multiple_of(rows * row, rows), rows + 2 * STEP)
+        return rdma(12, i, act.at[slot, some], act.at[slot, some], partner)
+
+    @pl.when(forms)
+    def _():
+        for i in range(2):
+            slot = 2 * (1 - chip) + i
+            pltpu.make_async_remote_copy(
+                src_ref=act.at[slot, inside], dst_ref=act.at[slot, inside],
+                send_sem=send_sem.at[7, 0], recv_sem=recv_sem.at[7, i],
+                device_id={"seq": partner}, device_id_type=MESH,
+            ).wait_recv()
+            act_hop(i, partner).start()
+
+    @pl.when(jnp.logical_not(forms))
+    def _():
+        for i in range(2):
+            act_hop(i, me).wait_recv()
+
+    for copy in (g_near, g_hop):
         copy.wait_recv()
 
-    pair = 2 * (me % 2)
+    pair = 2 * core
     whole = pl.ds(STEP, total)
     mine = merge(act[pair, whole], act[pair + 1, whole])
     mine = mine.T
@@ -415,27 +458,24 @@
     pl.when(has_prev)(lambda: up.wait_send())
     for copy in first + grads + spread + stats + inner + back + crossing:
         copy.wait_send()
-    for o, needs, full, piece in acts:
-        pl.when(needs)(lambda full=full: full.wait_send())
-        pl.when(jnp.logical_not(needs))(lambda piece=piece: piece.wait_send())
+    for copy in across + [act_across, act_near]:
+        copy.wait_send()
+
+    @pl.when(forms)
+    def _():
+        for i in range(2):
+            act_hop(i, partner).wait_send()
 
 
 def store_kernel(*refs):
-    count = (len(refs) - 1) // 2
-    copies = [
-        pltpu.make_async_copy(refs[i], refs[count + i], refs[-1].at[i]) for i in range(count)
-    ]
-    for copy in copies:
-        copy.start()
-    for copy in copies:
-        copy.wait()
+    for i in range(5):
+        refs[5 + i][...] = refs[i][...]
 
 
 def body(queries, key_rows, value_rows, conv_weight, output_gradient):
     rows, feats = queries.shape[1:]
     total = rows * N
     vmem = pl.BlockSpec(memory_space=pltpu.VMEM)
-    anyspace = pl.BlockSpec(memory_space=pl.ANY)
     shape = jax.ShapeDtypeStruct
     inside = lax.axis_size("dp") == 8
     gw_shape = (TAPS, 96, HEAD_DIM) if inside else (TAPS, 384, 384)
@@ -473,9 +513,11 @@
             pltpu.VMEM((2, N, 8, total), F32),
             pltpu.VMEM((3, total, WIN), BF16),
             pltpu.VMEM((N, 3, rows, WIN), BF16),
+            pltpu.VMEM((3, rows, 384), BF16),
+            pltpu.VMEM((rows, 384), BF16),
             pltpu.SemaphoreType.DMA((TAPS + 5,)),
-            pltpu.SemaphoreType.DMA((11, N)),
-            pltpu.SemaphoreType.DMA((11, N)),
+            pltpu.SemaphoreType.DMA((13, N)),
+            pltpu.SemaphoreType.DMA((13, N)),
         ] + (tail if inside else []),
         compiler_params=pltpu.CompilerParams(
             collective_id=0, has_side_effects=True, vmem_limit_bytes=int(62.5 * 2**20)
@@ -495,9 +537,8 @@
         outs = pl.pallas_call(
             store_kernel,
             out_shape=[shape(out.shape, out.dtype) for out in outs],
-            in_specs=[anyspace] * 5,
-            out_specs=[pl.BlockSpec(memory_space=pltpu.HBM)] * 5,
-            scratch_shapes=[pltpu.SemaphoreType.DMA((5,))],
+            in_specs=[vmem] * 5,
+            out_specs=[vmem] * 5,
             compiler_params=pltpu.CompilerParams(vmem_limit_bytes=int(62.5 * 2**20)),
         )(*outs)
     return (*(out[None] for out in outs[:4]), jnp.transpose(outs[4], (1, 0, 2)))

time: 88.9 us -> 53.9 us (0.61)
  Pallas kernels: 88.1 us -> 53.1 us
    pallas_call x1, Pallas kernels: 33.9 us -> 2.3 us  [body(): pl.pallas_call(store_kernel, out_shape=[shape(out.shape, out.dtype) for o...]
    pallas_call x1, Pallas kernels: 54.2 us -> 50.8 us  [body(): pl.pallas_call(kernel, out_shape=[shape((rows, feats), BF16)] * 4 + [shap...]
where the time goes in v3:
time: 53.9 us; the launch traced here: 53.7 us
  Pallas kernels  53.1 us (99%)
  between operations  0.64 us (1%)
    pallas_call x1, Pallas kernels, body(): pl.pallas_call(kernel, out_shape=[shape((rows, feats), BF16)] * 4 + [shap...  50.8 us
    pallas_call x1, Pallas kernels, body(): pl.pallas_call(store_kernel, out_shape=[shape(out.shape, out.dtype) for o...  2.3 us

profile of v3, /device:TPU:0, one launch (start us, length us, event | category | flops | bytes accessed | tf_op | source)
XLA Modules:
  0.0 53.7 jit_solution(10632248025142630466)
XLA Ops:
  0.6 50.8 %shard_map.92 = (bf16[128,768]{1,0:T(8,128)(2,1)}, bf16[128,768]{1,0:T(8,128)(2,1)}, bf16[128,768]{1,0:T(8,128)(2,1)}, bf16[128,768]{1,0:T(8,128)(2,1)}, f32[3,96,192]{2,1,0:T(8,128)}) custom-call(bf16[128,768]{1,0:T(8,128)(2,1)} %bitcast.11, bf16[128,768]{1,0:T(8,128)(2,1)} %bitcast.12, bf16[128,768]{1,0:T(8,128)(2,1)} %bitcast.13, ...), custom_call_target="tpu_custom_call" | custom-call | tf_op jit(solution)/shard_map/pallas_call | solution.py:496
  51.4 2.3 %shard_map.93 = (bf16[128,768]{1,0:T(8,128)(2,1)}, bf16[128,768]{1,0:T(8,128)(2,1)}, bf16[128,768]{1,0:T(8,128)(2,1)}, bf16[128,768]{1,0:T(8,128)(2,1)}, f32[3,96,192]{2,1,0:T(8,128)}) custom-call(bf16[128,768]{1,0:T(8,128)(2,1)} %get-tuple-element.15.refs_0_, bf16[128,768]{1,0:T(8,128)(2,1)} %get-tuple-element.16.refs_1_, ...), custom_call_target="tpu_custom_call" | custom-call | tf_op jit(solution)/shard_map/pallas_call | solution.py:537

commit v4 on v3

--- a/solution.py
+++ b/solution.py
@@ -283,6 +283,37 @@
         for i in range(2):
             act[2 * (1 - chip) + i, pl.ds(0, STEP)] = jnp.zeros((STEP, WIN), BF16)
             act[2 * (1 - chip) + i, pl.ds(STEP + total, STEP)] = jnp.zeros((STEP, WIN), BF16)
+
+    for copy in (g_near, g_hop):
+        copy.wait_recv()
+    act_near.wait_recv()
+    if tail:
+        gwf, xs, xr, zs, zo, zr, fin, x_send, x_recv, z_send, z_recv, c_sem = tail
+
+    def x_copy(t, j):
+        there = pl.ds(pl.multiple_of(96 * (2 * j + 1 - tx), 96), 96)
+        return pltpu.make_async_remote_copy(
+            src_ref=xs.at[t, there], dst_ref=xr.at[t, j],
+            send_sem=x_send.at[t, j], recv_sem=x_recv.at[t, j],
+            device_id={"dp": ring + 1 - 2 * tx}, device_id_type=MESH,
+        )
+
+    def form_gradient():
+        pair = 2 * core
+        mine = merge(act[pair, inside], act[pair + 1, inside])
+        mine = mine.T
+        scale = 1.0 / math.sqrt(total * lax.axis_size("dp"))
+        for t in range(TAPS):
+            term = nn(mine, gg[pl.ds((2 - t) * STEP, total)]) * scale
+            if not tail:
+                gw_ref[t] = term
+                continue
+            gwf[t] = term
+            xs[t] = term.astype(BF16)
+            for j in range(2):
+                x_copy(t, j).start()
+
+    pl.when(jnp.logical_not(forms))(form_gradient)
 
     for copy in inner:
         copy.wait_recv()
@@ -319,8 +350,6 @@
     for i in range(3):
         land[me, i] = dqkv[i, pl.ds(my_rows, rows)]
 
-    act_near.wait_recv()
-
     def act_hop(i, row):
         slot = 2 * (1 - chip) + i
         some = pl.ds(pl.multiple_of(rows * row, rows), rows + 2 * STEP)
@@ -336,40 +365,13 @@
                 device_id={"seq": partner}, device_id_type=MESH,
             ).wait_recv()
             act_hop(i, partner).start()
+        form_gradient()
 
     @pl.when(jnp.logical_not(forms))
     def _():
         for i in range(2):
             act_hop(i, me).wait_recv()
 
-    for copy in (g_near, g_hop):
-        copy.wait_recv()
-
-    pair = 2 * core
-    whole = pl.ds(STEP, total)
-    mine = merge(act[pair, whole], act[pair + 1, whole])
-    mine = mine.T
-    crossing = []
-    scale = 1.0 / math.sqrt(total * lax.axis_size("dp"))
-    for t in range(TAPS):
-        term = nn(mine, gg[pl.ds((2 - t) * STEP, total)])
-        term = term * scale
-        if not tail:
-            gw_ref[t] = term
-            continue
-        gwf, xs, xr, zs, zo, zr, fin, x_send, x_recv, z_send, z_recv, c_sem = tail
-        gwf[t] = term
-        xs[t] = term.astype(BF16)
-        for j in range(2):
-            there = pl.ds(pl.multiple_of(96 * (2 * j + 1 - tx), 96), 96)
-            copy = pltpu.make_async_remote_copy(
-                src_ref=xs.at[t, there], dst_ref=xr.at[t, j],
-                send_sem=x_send.at[t, j], recv_sem=x_recv.at[t, j],
-                device_id={"dp": ring + 1 - 2 * tx}, device_id_type=MESH,
-            )
-            copy.start()
-            crossing.append(copy)
-
     near = pl.ds(my_rows, rows + 2 * STEP)
     nearby = jnp.concatenate(
         [merge(act[0, near], act[1, near]), merge(act[2, near], act[3, near])], axis=1
@@ -379,23 +381,46 @@
     out += nn(nearby[2 * STEP :], w_ref[2])
     conv_ref[...] = out.astype(BF16)
 
-    along = []
+    step = tz + core * (3 - 2 * tz)
+    near_block, next_block = core, 1 - core
+
+    def z_copy(block, t, slot, goal):
+        there = goal + core * (3 - 2 * goal)
+        return pltpu.make_async_remote_copy(
+            src_ref=zo.at[block, t], dst_ref=zr.at[slot, t],
+            send_sem=z_send.at[t, block], recv_sem=z_recv.at[t, slot],
+            device_id={"dp": 2 * there + tx}, device_id_type=MESH,
+        )
+
     if tail:
         for t in range(TAPS):
             for j in range(2):
-                crossing[2 * t + j].wait_recv()
+                x_copy(t, j).wait_recv()
                 here = pl.ds(pl.multiple_of(96 * (2 * j + tx), 96), 96)
                 block = gwf[t, here] + xr[t, j].astype(F32)
                 zs[j, t] = block
                 zo[j, t] = block.astype(BF16)
-                target = 2 * core + j
-                copy = pltpu.make_async_remote_copy(
-                    src_ref=zo.at[j, t], dst_ref=zr.at[tz, t],
-                    send_sem=z_send.at[t, j], recv_sem=z_recv.at[t, tz],
-                    device_id={"dp": 2 * target + tx}, device_id_type=MESH,
-                )
-                pl.when(target != tz)(lambda copy=copy: copy.start())
-                along.append((target != tz, copy))
+
+            @pl.when(step == 3)
+            def _(t=t):
+                z_copy(0, t, 0, 2).start()
+                z_copy(1, t, 1, 2).start()
+
+            @pl.when(step == 2)
+            def _(t=t):
+                for j in range(2):
+                    z_copy(j, t, j, 2).wait_recv()
+                    zo[j, t] = (zs[j, t] + zr[j, t].astype(F32)).astype(BF16)
+                z_copy(near_block, t, 0, 0).start()
+                z_copy(next_block, t, 0, 1).start()
+
+            @pl.when(step == 1)
+            def _(t=t):
+                z_copy(near_block, t, 1, 0).start()
+
+            @pl.when(step == 0)
+            def _(t=t):
+                z_copy(next_block, t, 1, 1).start()
 
     for copy in back:
         copy.wait_recv()
@@ -405,7 +430,7 @@
         )
 
     if tail:
-        owner = tz // 2 == core
+        owner = step < 2
         other = 2 * (me // 2) + 1 - core
         lanes = pl.multiple_of(128 * (1 - core), 128)
         hand = [
@@ -431,14 +456,10 @@
         def _():
             for t in range(TAPS):
                 fin[t] = zs[tz % 2, t]
-                for o in (1, 2, 3):
-                    source = lax.rem(tz + o, 4)
-                    pltpu.make_async_remote_copy(
-                        src_ref=zo.at[0, t], dst_ref=zr.at[source, t],
-                        send_sem=z_send.at[t, 0], recv_sem=z_recv.at[t, source],
-                        device_id={"dp": 2 * source + tx}, device_id_type=MESH,
-                    ).wait_recv()
-                    fin[t] += zr[source, t].astype(F32)
+                z_copy(0, t, 0, 0).wait_recv()
+                fin[t] += zr[0, t].astype(F32)
+                z_copy(0, t, 1, 0).wait_recv()
+                fin[t] += zr[1, t].astype(F32)
                 hand[t].start()
             for copy in hand:
                 copy.wait_send()
@@ -451,12 +472,21 @@
         for t in range(TAPS):
             both = fin[t, :, pl.ds(mine_lanes, WIN)]
             gw_ref[t] = jnp.where(core == 0, both[:, :HEAD_DIM], both[:, WIN - HEAD_DIM :])
-        for go, copy in along:
-            pl.when(go)(lambda copy=copy: copy.wait_send())
+        for t in range(TAPS):
+
+            @pl.when(step >= 2)
+            def _(t=t):
+                for j in range(2):
+                    z_copy(j, t, 0, 0).wait_send()
+
+            pl.when(step == 1)(lambda t=t: z_copy(near_block, t, 1, 0).wait_send())
+            pl.when(step == 0)(lambda t=t: z_copy(next_block, t, 1, 1).wait_send())
+            for j in range(2):
+                x_copy(t, j).wait_send()
 
     pl.when(has_next)(lambda: down.wait_send())
     pl.when(has_prev)(lambda: up.wait_send())
-    for copy in first + grads + spread + stats + inner + back + crossing:
+    for copy in first + grads + spread + stats + inner + back:
         copy.wait_send()
     for copy in across + [act_across, act_near]:
         copy.wait_send()
@@ -485,12 +515,12 @@
         pltpu.VMEM((TAPS, 2, 96, 384), BF16),
         pltpu.VMEM((2, TAPS, 96, 384), F32),
         pltpu.VMEM((2, TAPS, 96, 384), BF16),
-        pltpu.VMEM((4, TAPS, 96, 384), BF16),
+        pltpu.VMEM((2, TAPS, 96, 384), BF16),
         pltpu.VMEM((TAPS, 96, 384), F32),
         pltpu.SemaphoreType.DMA((TAPS, 2)),
         pltpu.SemaphoreType.DMA((TAPS, 2)),
         pltpu.SemaphoreType.DMA((TAPS, 2)),
-        pltpu.SemaphoreType.DMA((TAPS, 4)),
+        pltpu.SemaphoreType.DMA((TAPS, 2)),
         pltpu.SemaphoreType.DMA((2, TAPS)),
     ]
     outs = pl.pallas_call(

time: 53.9 us -> 51.8 us (0.961)
  Pallas kernels: 53.1 us -> 51 us
    pallas_call x1, Pallas kernels: 50.8 us -> 48.7 us  [body(): pl.pallas_call(kernel, out_shape=[shape((rows, feats), BF16)] * 4 + [shap...]
where the time goes in v4:
time: 51.8 us; the launch traced here: 51.7 us
  Pallas kernels  51 us (98%)
  between operations  0.64 us (1%)
    pallas_call x1, Pallas kernels, body(): pl.pallas_call(kernel, out_shape=[shape((rows, feats), BF16)] * 4 + [shap...  48.7 us
    pallas_call x1, Pallas kernels, body(): pl.pallas_call(store_kernel, out_shape=[shape(out.shape, out.dtype) for o...  2.3 us

profile of v4, /device:TPU:0, one launch (start us, length us, event | category | flops | bytes accessed | tf_op | source)
XLA Modules:
  0.0 51.7 jit_solution(9751263828914865867)
XLA Ops:
  0.6 48.7 %shard_map.92 = (bf16[128,768]{1,0:T(8,128)(2,1)}, bf16[128,768]{1,0:T(8,128)(2,1)}, bf16[128,768]{1,0:T(8,128)(2,1)}, bf16[128,768]{1,0:T(8,128)(2,1)}, f32[3,96,192]{2,1,0:T(8,128)}) custom-call(bf16[128,768]{1,0:T(8,128)(2,1)} %bitcast.11, bf16[128,768]{1,0:T(8,128)(2,1)} %bitcast.12, bf16[128,768]{1,0:T(8,128)(2,1)} %bitcast.13, ...), custom_call_target="tpu_custom_call" | custom-call | tf_op jit(solution)/shard_map/pallas_call | solution.py:526
  49.4 2.3 %shard_map.93 = (bf16[128,768]{1,0:T(8,128)(2,1)}, bf16[128,768]{1,0:T(8,128)(2,1)}, bf16[128,768]{1,0:T(8,128)(2,1)}, bf16[128,768]{1,0:T(8,128)(2,1)}, f32[3,96,192]{2,1,0:T(8,128)}) custom-call(bf16[128,768]{1,0:T(8,128)(2,1)} %get-tuple-element.15.refs_0_, bf16[128,768]{1,0:T(8,128)(2,1)} %get-tuple-element.16.refs_1_, ...), custom_call_target="tpu_custom_call" | custom-call | tf_op jit(solution)/shard_map/pallas_call | solution.py:567

commit v5 on v4

--- a/solution.py
+++ b/solution.py
@@ -188,31 +188,39 @@
     mask32 = jnp.logical_and(lane >= low, lane < low + HEAD_DIM).astype(F32)
     mask = mask32.astype(BF16)
 
-    for i in range(3):
+    def arrive(i):
         across[i].wait_recv()
         copy = rdma(i, 3, xq.at[i, :, theirs_in_block], qkv.at[i, cross_rows], partner)
         copy.start()
         first.append(copy)
-    for i in range(3):
         qkv[i, cross_rows] = xq[i, :, mine_in_block]
-    for load in own:
-        load.wait()
-    for copy in first:
-        copy.wait_recv()
-    for i in range(3):
+        return copy
+
+    def settle(i, hop):
+        own[i].wait()
+        first[i].wait_recv()
+        hop.wait_recv()
         for b in range(N):
             part = pl.ds(b * rows, rows)
             qkv[i, part] = qkv[i, part] * mask
 
-    keys, values = qkv[1], qkv[2]
+    hops = [arrive(0), arrive(1)]
+    settle(0, hops[0])
+    settle(1, hops[1])
+    keys = qkv[1]
     for b in range(N):
         part = pl.ds(b * rows, rows)
         scores = nt(qkv[0, part], keys)
         top = jnp.max(scores, axis=-1, keepdims=True)
         expo = jnp.exp((scores - top) * inverse)
-        prob = expo * (1.0 / jnp.sum(expo, axis=-1, keepdims=True))
-        soft[part] = prob
-        out = nn(prob.astype(BF16), values).astype(BF16)
+        soft[part] = expo * (1.0 / jnp.sum(expo, axis=-1, keepdims=True))
+        if b == 1:
+            hops.append(arrive(2))
+    settle(2, hops[2])
+    values = qkv[2]
+    for b in range(N):
+        part = pl.ds(b * rows, rows)
+        out = nn(soft[part].astype(BF16), values).astype(BF16)
         att[part] = out
         wide = out.astype(F32)
         stat[0, me, :, b * rows : (b + 1) * rows] = as_row(
@@ -367,20 +375,6 @@
             act_hop(i, partner).start()
         form_gradient()
 
-    @pl.when(jnp.logical_not(forms))
-    def _():
-        for i in range(2):
-            act_hop(i, me).wait_recv()
-
-    near = pl.ds(my_rows, rows + 2 * STEP)
-    nearby = jnp.concatenate(
-        [merge(act[0, near], act[1, near]), merge(act[2, near], act[3, near])], axis=1
-    )
-    out = nn(nearby[:rows], w_ref[0])
-    out += nn(nearby[STEP : STEP + rows], w_ref[1])
-    out += nn(nearby[2 * STEP :], w_ref[2])
-    conv_ref[...] = out.astype(BF16)
-
     step = tz + core * (3 - 2 * tz)
     near_block, next_block = core, 1 - core
 
@@ -421,6 +415,20 @@
             @pl.when(step == 0)
             def _(t=t):
                 z_copy(next_block, t, 1, 1).start()
+
+    @pl.when(jnp.logical_not(forms))
+    def _():
+        for i in range(2):
+            act_hop(i, me).wait_recv()
+
+    near = pl.ds(my_rows, rows + 2 * STEP)
+    nearby = jnp.concatenate(
+        [merge(act[0, near], act[1, near]), merge(act[2, near], act[3, near])], axis=1
+    )
+    out = nn(nearby[:rows], w_ref[0])
+    out += nn(nearby[STEP : STEP + rows], w_ref[1])
+    out += nn(nearby[2 * STEP :], w_ref[2])
+    conv_ref[...] = out.astype(BF16)
 
     for copy in back:
         copy.wait_recv()

time: 51.8 us -> 48.8 us (0.942)
  the two profiles are of different devices: /device:TPU:0 before, /device:TPU:5 now
where the time goes in v5:
time: 48.8 us; the launch traced here: 48.7 us
  Pallas kernels  48 us (98%)
  between operations  0.64 us (1%)
    pallas_call x1, Pallas kernels, body(): pl.pallas_call(kernel, out_shape=[shape((rows, feats), BF16)] * 4 + [shap...  45.7 us
    pallas_call x1, Pallas kernels, body(): pl.pallas_call(store_kernel, out_shape=[shape(out.shape, out.dtype) for o...  2.3 us

profile of v5, /device:TPU:5, one launch (start us, length us, event | category | flops | bytes accessed | tf_op | source)
XLA Modules:
  0.0 48.7 jit_solution(10184563402999157709)
XLA Ops:
  0.6 45.7 %shard_map.92 = (bf16[128,768]{1,0:T(8,128)(2,1)}, bf16[128,768]{1,0:T(8,128)(2,1)}, bf16[128,768]{1,0:T(8,128)(2,1)}, bf16[128,768]{1,0:T(8,128)(2,1)}, f32[3,96,192]{2,1,0:T(8,128)}) custom-call(bf16[128,768]{1,0:T(8,128)(2,1)} %bitcast.11, bf16[128,768]{1,0:T(8,128)(2,1)} %bitcast.12, bf16[128,768]{1,0:T(8,128)(2,1)} %bitcast.13, ...), custom_call_target="tpu_custom_call" | custom-call | tf_op jit(solution)/shard_map/pallas_call | solution.py:534
  46.4 2.3 %shard_map.93 = (bf16[128,768]{1,0:T(8,128)(2,1)}, bf16[128,768]{1,0:T(8,128)(2,1)}, bf16[128,768]{1,0:T(8,128)(2,1)}, bf16[128,768]{1,0:T(8,128)(2,1)}, f32[3,96,192]{2,1,0:T(8,128)}) custom-call(bf16[128,768]{1,0:T(8,128)(2,1)} %get-tuple-element.15.refs_0_, bf16[128,768]{1,0:T(8,128)(2,1)} %get-tuple-element.16.refs_1_, ...), custom_call_target="tpu_custom_call" | custom-call | tf_op jit(solution)/shard_map/pallas_call | solution.py:575
